TPU v7x, 256 devices: a whole 4x4x8 slice. The times are simulated.
256 devices in a mesh: outer: 32 (over z, x_lo, core), inner: 8 (over y, x_hi).
Axes of the slice: x: 4 (x_hi: 2, x_lo: 2; x = x_hi * 2 + x_lo), y: 4, z: 8, core: 2. Of those that a mesh axis runs over, the one named last changes fastest.
Arguments:
- inputs: bfloat16 [65536, 8192], P(('outer', 'inner')), may hold values from -24 to 24
- queries: bfloat16 [65536, 4096], P(('outer', 'inner')), may hold values from -120 to 120
- key_rows: bfloat16 [65536, 512], P(('outer', 'inner')), may hold values from -16 to 16
- out_grad: bfloat16 [65536, 4096], P(('outer', 'inner')), may hold values from -0.29882812 to 0.29882812
- sel_blocks: int32 [1024, 16], P(('outer', 'inner')), may hold values from 0 to 31, as said below
- block_mask: int32 [1024, 16], P(('outer', 'inner')), may hold values from 0 to 1
Outputs:
- weight_grad: float32 [8192, 512], P(('inner', 'outer'))
Inputs may be any that keep to these rules, and one draw needn't show every extreme that they name: Row r of sel_blocks and block_mask belongs to query block r, at place b = r mod 32 in its sequence; the slots with block_mask 1 name distinct blocks numbered at most b, at most min(16, b + 1) of them, b itself always among them; slots with block_mask 0 may name any block of the sequence.
All inputs are finite; a program needn't handle non-finite values.
Results may differ from a plain program's by a relative error of at most 0.004.
Values may be sent and summed in bfloat16 or wider, within the bound.
A program may use at most 128 MiB of HBM per device.

v0:
```python
import math

import jax
import jax.numpy as jnp
from jax import lax
from jax.sharding import PartitionSpec as P

HD = 128
GROUP = 8
HK = 4
BLK = 64
SEL = 16


def block_contrib(query_block, grad_block, sequence_keys, chosen, usable, position, blocks):
    query_heads = query_block.reshape(BLK, HK, GROUP, HD)
    picked = sequence_keys.reshape(blocks, BLK, HK, HD)[chosen].reshape(SEL * BLK, HK, HD)
    factor = 1.0 / math.sqrt(HD)
    score = (
        jnp.einsum("qgrd,ngd->grqn", query_heads, picked, preferred_element_type=jnp.float32)
        * factor
    )
    slot_of = jnp.arange(SEL * BLK, dtype=jnp.int32) // BLK
    within = jnp.arange(SEL * BLK, dtype=jnp.int32) % BLK
    block_of = chosen[slot_of]
    open_slot = usable[slot_of] == 1
    query_pos = jnp.arange(BLK, dtype=jnp.int32)[:, None]
    allowed = open_slot[None, :] & (
        (block_of[None, :] < position)
        | (block_of[None, :] == position) & (within[None, :] <= query_pos)
    )
    masked = jnp.where(allowed[None, None], score, -1e30)
    row_max = jnp.max(masked, axis=-1, keepdims=True)
    weights = jnp.where(allowed[None, None], jnp.exp(masked - row_max), 0.0)
    probs = (weights / jnp.sum(weights, axis=-1, keepdims=True)).astype(jnp.bfloat16)
    grad_heads = grad_block.reshape(BLK, HK, GROUP, HD)
    contrib = jnp.einsum("grqn,qgrd->ngd", probs, grad_heads, preferred_element_type=jnp.float32)
    return contrib.reshape(SEL, BLK, HK * HD)


def body(inputs, queries, key_rows, out_grad, sel_blocks, block_mask):
    row_count = queries.shape[0]
    local_blocks = row_count // BLK
    value_width = key_rows.shape[1]
    sequence_keys = lax.all_gather(key_rows, "inner", axis=0, tiled=True)
    blocks = sequence_keys.shape[0] // BLK
    first_block = lax.axis_index("inner") * local_blocks

    def visit_block(running, block_item):
        query_block, grad_block, chosen, usable, offset = block_item
        contrib = block_contrib(
            query_block, grad_block, sequence_keys, chosen, usable, first_block + offset, blocks
        )
        return (running.at[chosen].add(contrib), None)

    start_value = jnp.zeros((blocks, BLK, value_width), jnp.float32)
    offsets = jnp.arange(local_blocks, dtype=jnp.int32)
    query_split = queries.reshape(local_blocks, BLK, queries.shape[1])
    grad_split = out_grad.reshape(local_blocks, BLK, out_grad.shape[1])
    running, _ = lax.scan(
        visit_block, start_value, (query_split, grad_split, sel_blocks, block_mask, offsets)
    )
    partial_grad = running.reshape(blocks * BLK, value_width)
    value_grad = lax.psum_scatter(partial_grad, "inner", scatter_dimension=0, tiled=True)
    value_low = value_grad.astype(jnp.bfloat16)
    outer_count = lax.axis_size("outer")
    inner_count = lax.axis_size("inner")
    model_width = inputs.shape[1]
    contract = (((0,), (0,)), ((), ()))
    owned = model_width // (outer_count * inner_count)
    arranged = (
        inputs.reshape(row_count, inner_count, outer_count, owned)
        .transpose(0, 2, 1, 3)
        .reshape(row_count, model_width)
    )
    return lax.psum_scatter(
        lax.dot_general(arranged, value_low, contract, preferred_element_type=jnp.float32),
        ("outer", "inner"),
        scatter_dimension=0,
        tiled=True,
    )


def solution(mesh):
    placed = (
        P(("outer", "inner"), None),
        P(("outer", "inner"), None),
        P(("outer", "inner"), None),
        P(("outer", "inner"), None),
        P(("outer", "inner"), None),
        P(("outer", "inner"), None),
    )
    return jax.shard_map(
        body, mesh=mesh, in_specs=placed, out_specs=P(("inner", "outer"), None), check_vma=False
    )
```

profile of v0, /device:TPU:1, one launch (start us, length us, event | category | flops | bytes accessed | tf_op | source)
XLA Modules:
  0.0 1690.1 jit_solution(4933625325890506331)
XLA Ops:
  7.3 65.1 %all-gather.2.cloned.1.call-done = bf16[2048,512]{1,0:T(8,128)(2,1)} async-done(((bf16[256,512]{1,0:T(8,128)(2,1)}), bf16[2048,512]{1,0:T(8,128)(2,1)}) %all-gather.2.cloned.1.call-update) | async-done | bytes 2097168 | tf_op jit(solution)/shard_map/all_gather | solution.py:45
  72.4 4.0 reshape.425
  76.4 2.5 broadcast_in_dim.44
  78.9 199.8 %while.13 = (s32[]{:T(128)}, f32[32,64,512]{2,1,0:T(8,128)}, s32[4,16]{1,0:T(4,128)}, bf16[4,64,4096]{2,1,0:T(8,128)(2,1)}, s32[4,16]{1,0:T(4,128)}, /*index=5*/...) while((s32[]{:T(128)}, f32[32,64,512]{2,1,0:T(8,128)}, ...), condition=%wide.wide.region_4.5_spmd, body=%wide.wide.region_0.4_spmd.sunk | while | flops 1089395712 | bytes 52647968 | solution.py:60
  82.0 0.7 fusion.65
  82.7 4.2 compare_select_fusion.18
  87.0 5.7 broadcast_compare_fusion.6
  92.7 0.7 fusion.66
  93.4 4.2 compare_select_fusion.19
  97.7 5.7 select_compare_fusion.3
  103.4 3.0 gather_fusion
  106.7 1.3 dynamic-slice_bitcast_fusion.4
  108.2 5.6 fusion.68
  113.8 4.0 divide_convert_fusion.3
  117.8 2.6 fusion.69
  120.5 1.9 copy.62
  122.3 2.1 reshape.441
  124.4 4.4 scatter_fusion
  131.9 0.7 fusion.65
  132.6 4.2 compare_select_fusion.18
  136.9 5.7 broadcast_compare_fusion.6
  142.6 0.7 fusion.66
  143.3 4.2 compare_select_fusion.19
  147.6 5.7 select_compare_fusion.3
  153.3 3.0 gather_fusion
  156.6 1.3 dynamic-slice_bitcast_fusion.4
  158.1 5.6 fusion.68
  163.7 4.0 divide_convert_fusion.3
  167.7 2.6 fusion.69
  170.4 1.9 copy.62
  172.2 2.1 reshape.441
  174.3 4.4 scatter_fusion
  181.8 0.7 fusion.65
  182.6 4.2 compare_select_fusion.18
  186.8 5.7 broadcast_compare_fusion.6
  192.5 0.7 fusion.66
  193.2 4.2 compare_select_fusion.19
  197.5 5.7 select_compare_fusion.3
  203.3 3.0 gather_fusion
  206.6 1.3 dynamic-slice_bitcast_fusion.4
  208.1 5.6 fusion.68
  213.6 4.0 divide_convert_fusion.3
  217.6 2.6 fusion.69
  220.3 1.9 copy.62
  222.2 2.1 reshape.441
  224.3 4.5 scatter_fusion
  232.6 4.2 compare_select_fusion.18
  236.8 5.7 broadcast_compare_fusion.6
  243.3 4.2 compare_select_fusion.19
  247.5 5.7 select_compare_fusion.3
  253.3 3.0 gather_fusion
  256.6 1.3 dynamic-slice_bitcast_fusion.4
  258.1 5.6 fusion.68
  263.7 4.0 divide_convert_fusion.3
  267.7 2.6 fusion.69
  270.3 1.9 copy.62
  272.2 2.1 reshape.441
  274.3 4.5 scatter_fusion
  279.0 6.4 copy.21
  285.4 4.8 copy.22
  290.2 76.4 %reduce-scatter.5.cloned.1.call-done = f32[256,512]{1,0:T(8,128)} async-done(((f32[2048,512]{1,0:T(8,128)}), f32[256,512]{1,0:T(8,128)}) %reduce-scatter.5.cloned.1.call-update) | async-done | bytes 524304 | tf_op jit(solution)/shard_map/reduce_scatter | solution.py:64
  366.6 10.5 convolution_bitcast_fusion
  377.1 17.5 %copy.25 = f32[8192,512]{1,0:T(8,128)} copy(f32[8192,512]{0,1:T(8,128)} %convolution_bitcast_fusion) | data formatting | bytes 33554432
  394.6 1289.0 %reduce-scatter.7.cloned.1.call-done = f32[32,512]{1,0:T(8,128)} async-done(((f32[8192,512]{1,0:T(8,128)}), f32[32,512]{1,0:T(8,128)}) %reduce-scatter.7.cloned.1.call-update) | async-done | bytes 65552 | tf_op jit(solution)/shard_map/reduce_scatter | solution.py:76
  (85 shorter events, 13.9 us)
Async XLA Ops:
  6.5 65.9 %all-gather.2.cloned.1.call-start = ((), (), s32[]{:S(2)}) async-start(), calls=%async_computation.2 | async-start | bytes 2359296 | tf_op jit(solution)/shard_map/all_gather | solution.py:45
  7.3 359.4 %reduce-scatter.5.cloned.1.call-start = ((), (), s32[]{:S(2)}) async-start(), calls=%async_computation.3 | async-start | bytes 4718592 | tf_op jit(solution)/shard_map/reduce_scatter | solution.py:64
  278.8 1404.8 %reduce-scatter.7.cloned.1.call-start = ((), (), s32[]{:S(2)}) async-start(), calls=%async_computation.4 | async-start | bytes 16842752 | tf_op jit(solution)/shard_map/reduce_scatter | solution.py:76
Sparse Core Ops, SparseCore 0:
  10.0 62.4 all-gather.1
  278.9 87.6 reduce-scatter.4
  394.7 1288.8 reduce-scatter.6
where the time goes:
time: 1700 us; the launch traced here: 1690 us
  waiting for transfers between devices  1430 us (84%)
  other arithmetic  118 us (7%)
  local copies, waits for them, and re-layouts  81.1 us (5%)
  matrix products  43.3 us (3%)
    reduce_scatter x1, waiting for transfers between devices, body(): lax.psum_scatter(lax.dot_general(arranged, value_low, contract, preferred...  1290 us
    reduce_scatter x1, waiting for transfers between devices, body(): lax.psum_scatter(partial_grad, 'inner', scatter_dimension=0, tiled=True)  76.4 us
    all_gather x1, waiting for transfers between devices, body(): sequence_keys = lax.all_gather(key_rows, 'inner', axis=0, tiled=True)  65.1 us
  transfers between devices with their start and end apart: 3, of which 3 were waited for; matrix products, arithmetic and copies ran while one was open for 1% of the time, Pallas kernels for 0%

commit v1 on v0

v1 whole, which is shorter than its diff:
```python
import math

import jax
import jax.numpy as jnp
from jax import lax
from jax.experimental import pallas as pl
from jax.experimental.pallas import tpu as pltpu
from jax.sharding import PartitionSpec as P

HD = 128
GROUP = 8
HK = 4
BLK = 64
SEL = 16
NB = 32
LB = 4
SCALE = math.log2(math.e) / math.sqrt(HD)
MESH = pl.DeviceIdType.MESH


def kernel(inputs, queries, key_rows, out_grad, sel, mask, out_ref, *scratch):
    scratch = list(scratch)

    def take(count):
        taken = scratch[:count]
        del scratch[:count]
        return taken

    keys = take(HK)
    give = take(HK)
    came = take(HK)
    value = take(HK)
    part = take(HK)
    part_in = take(HK)
    half = take(HK)
    half_in = take(HK)
    (q_ref, g_ref, x_ref, st_ref, contrib, bias, vacc, hacc, inverse) = take(9)
    (loc, key_s, key_r, x_s, x_r, give_s, give_r, val_s, val_r, p1_s, p1_r, p2_s, p2_r) = take(13)

    outer, inner = lax.axis_index("outer"), lax.axis_index("inner")
    core, xlo, z = lax.rem(outer, 2), lax.rem(outer // 2, 2), outer // 4
    y, xhi = inner // 2, lax.rem(inner, 2)
    slot = y * 2 + core

    def device(z_, xlo_, core_, y_, xhi_):
        return (z_ * 4 + xlo_ * 2 + core_, y_ * 2 + xhi_)

    def flip(value_, bit):
        return 1 - value_ if bit else value_

    def remote(src, dst, send, recv, target):
        return pltpu.make_async_remote_copy(
            src_ref=src, dst_ref=dst, send_sem=send, recv_sem=recv, device_id=target, device_id_type=MESH
        )

    q_loads = [
        pltpu.make_async_copy(
            queries.at[:, :, pl.ds(g * 1024, 1024)], q_ref.at[g], loc.at[0, g]
        )
        for g in range(HK)
    ]
    g_loads = [
        pltpu.make_async_copy(
            out_grad.at[:, :, pl.ds(g * 1024, 1024)], g_ref.at[g], loc.at[1, g]
        )
        for g in range(HK)
    ]
    k_loads = [
        pltpu.make_async_copy(
            key_rows.at[:, :, pl.ds(g * HD, HD)], keys[g].at[pl.ds(inner * LB, LB)], loc.at[2, g]
        )
        for g in range(HK)
    ]
    x_load = pltpu.make_async_copy(
        inputs.at[:, pl.ds(pl.multiple_of(slot * 1024, 1024), 1024)], x_ref.at[slot], loc.at[3, 0]
    )
    for g in range(HK):
        k_loads[g].start()
        q_loads[g].start()
        g_loads[g].start()

    barrier = pltpu.get_barrier_semaphore()

    def greet(target):
        pl.semaphore_signal(barrier, inc=1, device_id=target, device_id_type=MESH)

    for d in range(1, 8):
        greet((outer, lax.rem(inner + d, 8)))
    for dy in range(4):
        greet(device(z, xlo, 1 - core, lax.rem(y + dy, 4), xhi))
    for fl, fc, fh in ((0, 1, 1), (1, 0, 0), (1, 0, 1), (1, 1, 0), (1, 1, 1)):
        greet(device(z, flip(xlo, fl), flip(core, fc), y, flip(xhi, fh)))
    for d in range(1, 8):
        greet(device(lax.rem(z + d, 8), xlo, core, y, xhi))
    pl.semaphore_wait(barrier, 23)

    def key_copy(g, d):
        return remote(
            key_rows.at[:, :, pl.ds(g * HD, HD)],
            keys[g].at[pl.ds(inner * LB, LB)],
            key_s.at[g, d],
            key_r.at[g, d],
            (outer, lax.rem(inner + d, 8)),
        )

    def key_arrival(g, d):
        src = lax.rem(inner + 8 - d, 8)
        return remote(
            key_rows.at[:, :, pl.ds(g * HD, HD)],
            keys[g].at[pl.ds(src * LB, LB)],
            key_s.at[g, d],
            key_r.at[g, d],
            (outer, src),
        )

    for g in range(HK):
        for d in range(1, 8):

            @pl.when(inner + d < 8)
            def _():
                key_copy(g, d).start()

    spread = [(dy, dc) for dy in range(4) for dc in range(2) if (dy, dc) != (0, 0)]

    def peer(dy, dc):
        return lax.rem(y + dy, 4), flip(core, dc)

    def source(dy, dc):
        return lax.rem(y + 4 - dy, 4), flip(core, dc)

    def x_copy(dy, dc):
        py, pc = peer(dy, dc)
        return remote(
            inputs.at[:, pl.ds(pl.multiple_of((py * 2 + pc) * 1024, 1024), 1024)],
            x_ref.at[slot],
            x_s.at[dy * 2 + dc],
            x_r.at[dy * 2 + dc],
            device(z, xlo, pc, py, xhi),
        )

    def x_arrival(dy, dc):
        sy, sc = source(dy, dc)
        return remote(
            inputs.at[:, pl.ds(0, 1024)],
            x_ref.at[sy * 2 + sc],
            x_s.at[dy * 2 + dc],
            x_r.at[dy * 2 + dc],
            device(z, xlo, sc, sy, xhi),
        )

    x_load.start()
    for dy, dc in spread:
        x_copy(dy, dc).start()

    def invert(kb, carry):
        for qb in range(LB):
            found = jnp.int32(SEL)
            for s in range(SEL):
                found = jnp.where((mask[qb, s] == 1) & (sel[qb, s] == kb), jnp.int32(s), found)
            inverse[qb, kb] = found
        return carry

    lax.fori_loop(0, inner * LB + LB, invert, 0)
    key_at = lax.broadcasted_iota(jnp.int32, (BLK, HD), 0)
    query_at = lax.rem(lax.broadcasted_iota(jnp.int32, (BLK, HD), 1), BLK)
    bias[0] = jnp.zeros((BLK, HD), jnp.float32)
    bias[1] = jnp.where(key_at <= query_at, 0.0, -1e30).astype(jnp.float32)
    bias[2] = jnp.full((BLK, HD), -1e30, jnp.float32)
    for qb in range(LB):
        contrib[qb, SEL] = jnp.zeros((BLK, HD), jnp.float32)

    def heads(ref, g, qb):
        return jnp.concatenate([ref[g, qb, :, pl.ds(h * HD, HD)] for h in range(GROUP)], axis=0)

    def attend(g):
        def one(qb, carry):
            place = inner * LB + qb
            query = heads(q_ref, g, qb)
            top = jnp.full((8, GROUP * BLK), -3e38, jnp.float32)
            for quad in range(4):
                picked, masks = [], []
                for s in range(4 * quad, 4 * quad + 4):
                    used = mask[qb, s] == 1
                    block = sel[qb, s]
                    picked.append(keys[g][jnp.where(used, block, place)])
                    kind = jnp.where(used, jnp.where(block == place, 1, 0), 2)
                    masks.append(bias[kind])
                scores = lax.dot_general(
                    jnp.concatenate(picked, axis=0),
                    query,
                    (((1,), (1,)), ((), ())),
                    preferred_element_type=jnp.float32,
                )
                shift = jnp.concatenate(masks, axis=0)
                scores = scores + jnp.concatenate([shift] * 4, axis=1)
                st_ref[quad] = scores
                top = jnp.maximum(top, jnp.max(scores.reshape(32, 8, GROUP * BLK), axis=0))
            top = jnp.max(top, axis=0, keepdims=True)
            total = jnp.zeros((8, GROUP * BLK), jnp.float32)
            for quad in range(4):
                weights = jnp.exp2((st_ref[quad] - top) * SCALE)
                st_ref[quad] = weights
                total = total + jnp.sum(weights.reshape(32, 8, GROUP * BLK), axis=0)
            norm = 1.0 / jnp.sum(total, axis=0, keepdims=True)
            grad = heads(g_ref, g, qb)
            for quad in range(4):
                probs = (st_ref[quad] * norm).astype(jnp.bfloat16)
                done = jnp.dot(probs, grad, preferred_element_type=jnp.float32)
                contrib[qb, pl.ds(4 * quad, 4)] = done.reshape(4, BLK, HD)
            return carry

        lax.fori_loop(0, LB, one, 0)

    def give_copy(g, j):
        d = inner - j
        return remote(
            give[g].at[j], came[g].at[d - 1], give_s.at[g, d], give_r.at[g, d], (outer, j)
        )

    def give_arrival(g, d):
        src = lax.rem(inner + d, 8)
        return remote(
            give[g].at[src], came[g].at[d - 1], give_s.at[g, d], give_r.at[g, d], (outer, src)
        )

    def hand_out(g):
        def owner(j, carry):
            for t in range(LB):
                terms = [contrib[qb, inverse[qb, j * LB + t]] for qb in range(LB)]
                give[g][j, t] = (terms[0] + terms[1]) + (terms[2] + terms[3])

            @pl.when(j < inner)
            def _():
                give_copy(g, j).start()

            return carry

        lax.fori_loop(0, inner + 1, owner, 0)

    def value_copy(g, dy, dc):
        py, pc = peer(dy, dc)
        return remote(
            value[g].at[slot],
            value[g].at[slot],
            val_s.at[g, dy * 2 + dc],
            val_r.at[g, dy * 2 + dc],
            device(z, xlo, pc, py, xhi),
        )

    def value_arrival(g, dy, dc):
        sy, sc = source(dy, dc)
        return remote(
            value[g].at[sy * 2 + sc],
            value[g].at[sy * 2 + sc],
            val_s.at[g, dy * 2 + dc],
            val_r.at[g, dy * 2 + dc],
            device(z, xlo, sc, sy, xhi),
        )

    def own(g):
        vacc[...] = give[g][inner]
        for d in range(1, 8):

            @pl.when(inner + d < 8)
            def _():
                give_arrival(g, d).wait_recv()
                vacc[...] += came[g][d - 1]

        value[g][slot] = vacc[...].reshape(LB * BLK, HD).astype(jnp.bfloat16)
        for dy, dc in spread:
            value_copy(g, dy, dc).start()

    def part_copy(g, fl, fc):
        k = flip(xlo, fl) * 2 + flip(core, fc)
        return remote(
            part[g].at[:, k],
            part_in[g].at[xhi * 2 + xlo],
            p1_s.at[g, fl * 2 + fc],
            p1_r.at[g, xhi * 2 + xlo],
            device(z, flip(xlo, fl), flip(core, fc), y, core),
        )

    def part_arrival(g, src_hi, src_lo):
        return remote(
            part[g].at[:, 0],
            part_in[g].at[src_hi * 2 + src_lo],
            p1_s.at[g, 0],
            p1_r.at[g, src_hi * 2 + src_lo],
            device(z, src_lo, xhi, y, src_hi),
        )

    def multiply(g):
        for dy, dc in spread:
            value_arrival(g, dy, dc).wait_recv()
        low = value[g][...].reshape(8 * LB * BLK, HD)
        for tile in range(4):
            wide = x_ref[:, :, pl.ds(tile * 256, 256)].reshape(8 * LB * BLK, 256)
            term = lax.dot_general(
                low, wide, (((0,), (0,)), ((), ())), preferred_element_type=jnp.float32
            )
            part[g][pl.ds(2 * tile, 2)] = term.T.astype(jnp.bfloat16).reshape(2, 4, 32, HD)
        for fl in range(2):
            for fc in range(2):
                if (fl, fc) == (0, 0):

                    @pl.when(xhi != core)
                    def _():
                        part_copy(g, 0, 0).start()

                    @pl.when(xhi == core)
                    def _():
                        part_in[g][xhi * 2 + xlo] = part[g][:, xlo * 2 + core]

                else:
                    part_copy(g, fl, fc).start()

    def half_copy(g, d):
        to = lax.rem(z + d, 8)
        return remote(
            half[g].at[to],
            half_in[g].at[d - 1],
            p2_s.at[g, d],
            p2_r.at[g, d],
            device(to, xlo, core, y, xhi),
        )

    def half_arrival(g, d):
        src = lax.rem(z + 8 - d, 8)
        return remote(
            half[g].at[src],
            half_in[g].at[d - 1],
            p2_s.at[g, d],
            p2_r.at[g, d],
            device(src, xlo, core, y, xhi),
        )

    def shrink(g):
        for src_hi in range(2):
            for src_lo in range(2):

                @pl.when((src_hi != xhi) | (src_lo != xlo) | (core != xhi))
                def _():
                    part_arrival(g, src_hi, src_lo).wait_recv()

        terms = [part_in[g][k].astype(jnp.float32) for k in range(4)]
        hacc[g] = (terms[0] + terms[1]) + (terms[2] + terms[3])
        half[g][...] = hacc[g].astype(jnp.bfloat16)
        for d in range(1, 8):
            half_copy(g, d).start()

    def finish(g):
        total = hacc[g, z]
        for d in range(1, 8):
            half_arrival(g, d).wait_recv()
            total = total + half_in[g][d - 1].astype(jnp.float32)
        out_ref[:, pl.ds(g * HD, HD)] = total

    def start_of(g):
        k_loads[g].wait()
        q_loads[g].wait()
        g_loads[g].wait()
        for d in range(1, 8):

            @pl.when(inner - d >= 0)
            def _():
                key_arrival(g, d).wait_recv()

    start_of(0)
    attend(0)
    hand_out(0)
    start_of(1)
    attend(1)
    hand_out(1)
    own(0)
    start_of(2)
    attend(2)
    hand_out(2)
    own(1)
    start_of(3)
    attend(3)
    hand_out(3)
    own(2)
    x_load.wait()
    for dy, dc in spread:
        x_arrival(dy, dc).wait_recv()
    multiply(0)
    own(3)
    multiply(1)
    shrink(0)
    multiply(2)
    shrink(1)
    multiply(3)
    shrink(2)
    shrink(3)
    for g in range(HK):
        finish(g)

    for g in range(HK):
        for d in range(1, 8):

            @pl.when(inner + d < 8)
            def _():
                key_copy(g, d).wait_send()

            @pl.when(inner - d >= 0)
            def _():
                give_copy(g, inner - d).wait_send()

            half_copy(g, d).wait_send()
        for dy, dc in spread:
            value_copy(g, dy, dc).wait_send()
        for fl in range(2):
            for fc in range(2):
                if (fl, fc) == (0, 0):

                    @pl.when(xhi != core)
                    def _():
                        part_copy(g, 0, 0).wait_send()

                else:
                    part_copy(g, fl, fc).wait_send()
    for dy, dc in spread:
        x_copy(dy, dc).wait_send()


def body(inputs, queries, key_rows, out_grad, sel_blocks, block_mask):
    any_ref = pl.BlockSpec(memory_space=pl.ANY)
    smem = pl.BlockSpec(memory_space=pltpu.SMEM)
    bf16, f32 = jnp.bfloat16, jnp.float32
    dma = pltpu.SemaphoreType.DMA
    scratch = (
        [pltpu.VMEM((NB, BLK, HD), bf16)] * HK
        + [pltpu.VMEM((8, LB, BLK, HD), f32)] * HK
        + [pltpu.VMEM((7, LB, BLK, HD), f32)] * HK
        + [pltpu.VMEM((8, LB * BLK, HD), bf16)] * HK
        + [pltpu.VMEM((8, 4, 32, HD), bf16)] * HK
        + [pltpu.VMEM((4, 8, 32, HD), bf16)] * HK
        + [pltpu.VMEM((8, 32, HD), bf16)] * HK
        + [pltpu.VMEM((7, 32, HD), bf16)] * HK
        + [
            pltpu.VMEM((HK, LB, BLK, 1024), bf16),
            pltpu.VMEM((HK, LB, BLK, 1024), bf16),
            pltpu.VMEM((8, LB * BLK, 1024), bf16),
            pltpu.VMEM((4, 256, GROUP * BLK), f32),
            pltpu.VMEM((LB, SEL + 1, BLK, HD), f32),
            pltpu.VMEM((3, BLK, HD), f32),
            pltpu.VMEM((LB, BLK, HD), f32),
            pltpu.VMEM((HK, 8, 32, HD), f32),
            pltpu.SMEM((LB, NB), jnp.int32),
        ]
        + [
            dma((4, HK)),
            dma((HK, 8)),
            dma((HK, 8)),
            dma((8,)),
            dma((8,)),
            dma((HK, 8)),
            dma((HK, 8)),
            dma((HK, 8)),
            dma((HK, 8)),
            dma((HK, 4)),
            dma((HK, 4)),
            dma((HK, 8)),
            dma((HK, 8)),
        ]
    )
    return pl.pallas_call(
        kernel,
        out_shape=jax.ShapeDtypeStruct((32, HK * HD), f32),
        in_specs=[any_ref, any_ref, any_ref, any_ref, smem, smem],
        out_specs=pl.BlockSpec(memory_space=pltpu.VMEM),
        scratch_shapes=scratch,
        compiler_params=pltpu.CompilerParams(
            collective_id=0, has_side_effects=True, vmem_limit_bytes=56 * 1024 * 1024
        ),
        cost_estimate=pl.CostEstimate(
            flops=6_500_000_000, bytes_accessed=9_000_000, transcendentals=8_400_000
        ),
    )(
        inputs,
        queries.reshape(LB, BLK, 4096),
        key_rows.reshape(LB, BLK, 512),
        out_grad.reshape(LB, BLK, 4096),
        sel_blocks,
        block_mask,
    )


def solution(mesh):
    placed = P(("outer", "inner"), None)
    return jax.shard_map(
        body, mesh=mesh, in_specs=(placed,) * 6, out_specs=P(("inner", "outer"), None), check_vma=False
    )
```

time: 1700 us -> 147 us (0.09)
  waiting for transfers between devices: 1430 us -> 0 us
  Pallas kernels: 0 us -> 146 us
  other arithmetic: 118 us -> 0 us
  local copies, waits for them, and re-layouts: 81.1 us -> 1.47 us
  matrix products: 43.3 us -> 0 us
    reduce_scatter x2 -> x0, waiting for transfers between devices: 1370 us -> none  [the longest x1 1290 us: body(): lax.psum_scatter(lax.dot_general(arranged, value_low, contract, preferred...]
    pallas_call x0 -> x1, Pallas kernels: none -> 146 us  [body(): pl.pallas_call(kernel, out_shape=jax.ShapeDtypeStruct((32, HK * HD), f32)...]
    all_gather x1 -> x0, waiting for transfers between devices: 65.1 us -> none  [body(): sequence_keys = lax.all_gather(key_rows, 'inner', axis=0, tiled=True)]
    gather x48 -> x0, other arithmetic: 35.2 us -> none  [the longest x40 18.2 us: block_contrib(): open_slot = usable[slot_of] == 1]
    eq x8 -> x0, other arithmetic: 22.8 us -> none  [the longest x4 22.8 us: block_contrib(): open_slot = usable[slot_of] == 1]
    lt x4 -> x0, other arithmetic: 22.8 us -> none  [block_contrib(): block_of[None, :] < position]
    unnamed x2 -> x1, local copies, waits for them, and re-layouts: 23.9 us -> 1.47 us
    sub x4 -> x0, matrix products: 22.3 us -> none  [block_contrib(): weights = jnp.where(allowed[None, None], jnp.exp(masked - row_max), 0.0)]
  transfers between devices with their start and end apart: 3 -> 0, of which waited for: 3 -> 0; matrix products, arithmetic and copies ran while one was open for 1% -> 0% of each run, Pallas kernels for 0% -> 0%
where the time goes in v1:
time: 147 us
  Pallas kernels  146 us (99%)
  local copies, waits for them, and re-layouts  1.47 us (1%)
    pallas_call x1, Pallas kernels, body(): pl.pallas_call(kernel, out_shape=jax.ShapeDtypeStruct((32, HK * HD), f32)...  146 us

profile of v1, /device:TPU:1, one launch (start us, length us, event | category | flops | bytes accessed | tf_op | source)
XLA Modules:
  0.0 147.2 jit_solution(15350048370053420010)
XLA Ops:
  0.0 145.7 %shard_map.64 = f32[32,512]{1,0:T(8,128)} custom-call(bf16[256,8192]{1,0:T(8,128)(2,1)} %inputs.1, bf16[4,64,4096]{2,1,0:T(8,128)(2,1)} %bitcast.3, bf16[4,64,512]{2,1,0:T(8,128)(2,1)} %bitcast.5, bf16[4,64,4096]{2,1,0:T(8,128)(2,1)} %bitcast.4, s32[4,16]{1,0:T(4,128)} %sel.1, s32[4,16]{1,0:T(4,128)} %mask.1), custom_call_target="tpu_custom_call" | custom-call | flops 6499999744 | bytes 9000000 | tf_op jit(solution)/shard_map/pallas_call | solution.py:467
  145.7 1.5 %copy.8 = f32[32,512]{1,0:T(8,128)} copy(f32[32,512]{1,0:T(8,128)} %shard_map.64) | data formatting | bytes 131072

commit v2 on v1

v2 whole, which is shorter than its diff:
```python
import math

import jax
import jax.numpy as jnp
from jax import lax
from jax.experimental import pallas as pl
from jax.experimental.pallas import tpu as pltpu
from jax.sharding import PartitionSpec as P

HD = 128
GROUP = 8
HK = 4
BLK = 64
SEL = 16
NB = 32
LB = 4
SCALE = math.log2(math.e) / math.sqrt(HD)
MESH = pl.DeviceIdType.MESH
MID = jnp.bfloat16


def kernel(inputs, queries, key_rows, out_grad, sel, mask, out_ref, *scratch):
    scratch = list(scratch)

    def take(count):
        taken = scratch[:count]
        del scratch[:count]
        return taken

    keys = take(HK)
    give = take(HK)
    came = take(HK)
    value = take(HK)
    part = take(HK)
    part_in = take(HK)
    mid = take(HK)
    mid_in = take(HK)
    low = take(HK)
    low_in = take(HK)
    (q_ref, g_ref, xa_ref, xb_ref, st_ref, contrib, bias, vacc, inverse) = take(9)
    (loc, key_s, key_r, xa_s, xa_r, xb_s, xb_r, give_s, give_r, val_s, val_r) = take(11)
    (p1_s, p1_r, p2_s, p2_r, p3_s, p3_r) = take(6)

    outer, inner = lax.axis_index("outer"), lax.axis_index("inner")
    core, xlo, z = lax.rem(outer, 2), lax.rem(outer // 2, 2), outer // 4
    y, xhi = inner // 2, lax.rem(inner, 2)
    x, zl, zh = xhi * 2 + xlo, lax.rem(z, 2), z // 2
    member = zl * 2 + core

    def device(z_, xlo_, core_, y_, xhi_):
        return (z_ * 4 + xlo_ * 2 + core_, y_ * 2 + xhi_)

    def across(x_):
        return device(z, lax.rem(x_, 2), core, y, x_ // 2)

    def mate(dz, dc):
        return (1 - zl if dz else zl), (1 - core if dc else core)

    def remote(src, dst, send, recv, target):
        return pltpu.make_async_remote_copy(
            src_ref=src, dst_ref=dst, send_sem=send, recv_sem=recv, device_id=target, device_id_type=MESH
        )

    barrier = pltpu.get_barrier_semaphore()

    def greet(target):
        pl.semaphore_signal(barrier, inc=1, device_id=target, device_id_type=MESH)

    for dz in (4, 3, 5, 2, 6):
        for dc in range(2):
            greet(device(lax.rem(z + dz, 8), xlo, (1 - core if dc else core), y, xhi))
    for d in range(1, 8):
        greet((outer, lax.rem(inner + d, 8)))
    for dz, dc in ((1, 0), (1, 1), (7, 0), (7, 1), (0, 1)):
        greet(device(lax.rem(z + dz, 8), xlo, (1 - core if dc else core), y, xhi))
    for dx in (1, 3):
        greet(across(lax.rem(x + dx, 4)))

    q_loads = [
        pltpu.make_async_copy(
            queries.at[:, :, pl.ds(g * 1024, 1024)], q_ref.at[g], loc.at[0, g]
        )
        for g in range(HK)
    ]
    g_loads = [
        pltpu.make_async_copy(
            out_grad.at[:, :, pl.ds(g * 1024, 1024)], g_ref.at[g], loc.at[1, g]
        )
        for g in range(HK)
    ]
    k_loads = [
        pltpu.make_async_copy(
            key_rows.at[:, :, pl.ds(g * HD, HD)], keys[g].at[pl.ds(inner * LB, LB)], loc.at[2, g]
        )
        for g in range(HK)
    ]
    def columns_a(blk, m):
        return inputs.at[:, pl.ds(pl.multiple_of(blk * 1024 + (m // 2) * 512 + (m % 2) * 128, 128), 128)]

    def columns_b(blk, c):
        return inputs.at[:, pl.ds(pl.multiple_of(blk * 1024 + 256 + c * 512, 256), 256)]

    x_loads = []
    for blk in range(8):
        x_loads += [
            pltpu.make_async_copy(columns_a(blk, member), xa_ref.at[blk, member], loc.at[3, blk]),
            pltpu.make_async_copy(columns_b(blk, core), xb_ref.at[blk, core], loc.at[4, blk]),
        ]
    for g in range(HK):
        k_loads[g].start()
        q_loads[g].start()
        g_loads[g].start()

    pl.semaphore_wait(barrier, 24)

    def key_copy(g, d):
        return remote(
            key_rows.at[:, :, pl.ds(g * HD, HD)],
            keys[g].at[pl.ds(inner * LB, LB)],
            key_s.at[g, d],
            key_r.at[g, d],
            (outer, lax.rem(inner + d, 8)),
        )

    def key_arrival(g, d):
        src = lax.rem(inner + 8 - d, 8)
        return remote(
            key_rows.at[:, :, pl.ds(g * HD, HD)],
            keys[g].at[pl.ds(src * LB, LB)],
            key_s.at[g, d],
            key_r.at[g, d],
            (outer, src),
        )

    def key_goes(d):
        return inner + d < 8

    def key_comes(d):
        return inner - d >= 0

    def send_keys(g):
        for d in range(1, 8):

            @pl.when(key_goes(d))
            def _():
                key_copy(g, d).start()

    send_keys(0)

    mates = [(0, 1), (1, 0), (1, 1)]

    def xa_copy(blk, dz, dc):
        pz, pc = mate(dz, dc)
        return remote(
            columns_a(blk, pz * 2 + pc),
            xa_ref.at[blk, member],
            xa_s.at[dz * 2 + dc, blk],
            xa_r.at[dz * 2 + dc, blk],
            device(zh * 2 + pz, xlo, pc, y, xhi),
        )

    def xa_arrival(blk, dz, dc):
        sz, sc = mate(dz, dc)
        return remote(
            columns_a(blk, member),
            xa_ref.at[blk, sz * 2 + sc],
            xa_s.at[dz * 2 + dc, blk],
            xa_r.at[dz * 2 + dc, blk],
            device(zh * 2 + sz, xlo, sc, y, xhi),
        )

    def xb_copy(blk):
        return remote(
            columns_b(blk, 1 - core),
            xb_ref.at[blk, core],
            xb_s.at[blk],
            xb_r.at[blk],
            device(z, xlo, 1 - core, y, xhi),
        )

    def xb_arrival(blk):
        return remote(
            columns_b(blk, core),
            xb_ref.at[blk, 1 - core],
            xb_s.at[blk],
            xb_r.at[blk],
            device(z, xlo, 1 - core, y, xhi),
        )

    for dz, dc in mates[::-1]:
        for blk in range(8):
            xa_copy(blk, dz, dc).start()
    for blk in range(8):
        xb_copy(blk).start()
    for load in x_loads:
        load.start()

    for qb in range(LB):
        named = [jnp.where(mask[qb, s] == 1, sel[qb, s], -1) for s in range(SEL)]

        def invert(kb, carry):
            found = jnp.int32(SEL)
            for s in range(SEL):
                found = jnp.where(named[s] == kb, jnp.int32(s), found)
            inverse[qb, kb] = found
            return carry

        lax.fori_loop(0, inner * LB + LB, invert, 0)
    key_at = lax.broadcasted_iota(jnp.int32, (BLK, HD), 0)
    query_at = lax.rem(lax.broadcasted_iota(jnp.int32, (BLK, HD), 1), BLK)
    bias[0] = jnp.zeros((BLK, HD), jnp.float32)
    bias[1] = jnp.where(key_at <= query_at, 0.0, -1e30).astype(jnp.float32)
    bias[2] = jnp.full((BLK, HD), -1e30, jnp.float32)
    for qb in range(LB):
        contrib[qb, SEL] = jnp.zeros((BLK, HD), jnp.float32)

    def heads(ref, g, qb):
        return jnp.concatenate([ref[g, qb, :, pl.ds(h * HD, HD)] for h in range(GROUP)], axis=0)

    def attend(g):
        def one(qb, carry):
            place = inner * LB + qb
            query = heads(q_ref, g, qb)
            top = jnp.full((8, GROUP * BLK), -3e38, jnp.float32)
            for quad in range(4):
                picked, masks = [], []
                for s in range(4 * quad, 4 * quad + 4):
                    used = mask[qb, s] == 1
                    block = sel[qb, s]
                    picked.append(keys[g][jnp.where(used, block, place)])
                    kind = jnp.where(used, jnp.where(block == place, 1, 0), 2)
                    masks.append(bias[kind])
                scores = lax.dot_general(
                    jnp.concatenate(picked, axis=0),
                    query,
                    (((1,), (1,)), ((), ())),
                    preferred_element_type=jnp.float32,
                )
                shift = jnp.concatenate(masks, axis=0)
                scores = scores + jnp.concatenate([shift] * 4, axis=1)
                st_ref[quad] = scores
                top = jnp.maximum(top, jnp.max(scores.reshape(32, 8, GROUP * BLK), axis=0))
            top = jnp.max(top, axis=0, keepdims=True)
            total = jnp.zeros((8, GROUP * BLK), jnp.float32)
            for quad in range(4):
                weights = jnp.exp2((st_ref[quad] - top) * SCALE)
                st_ref[quad] = weights
                total = total + jnp.sum(weights.reshape(32, 8, GROUP * BLK), axis=0)
            norm = 1.0 / jnp.sum(total, axis=0, keepdims=True)
            grad = heads(g_ref, g, qb)
            for quad in range(4):
                probs = (st_ref[quad] * norm).astype(jnp.bfloat16)
                done = jnp.dot(probs, grad, preferred_element_type=jnp.float32)
                contrib[qb, pl.ds(4 * quad, 4)] = done.reshape(4, BLK, HD)
            return carry

        lax.fori_loop(0, LB, one, 0)

    def give_copy(g, j):
        d = inner - j
        return remote(
            give[g].at[j], came[g].at[d - 1], give_s.at[g, d], give_r.at[g, d], (outer, j)
        )

    def give_arrival(g, d):
        src = lax.rem(inner + d, 8)
        return remote(
            give[g].at[src], came[g].at[d - 1], give_s.at[g, d], give_r.at[g, d], (outer, src)
        )

    def terms_of(kb):
        terms = [contrib[qb, inverse[qb, kb]] for qb in range(LB)]
        return (terms[0] + terms[1]) + (terms[2] + terms[3])

    def hand_out(g):
        def owner(j, carry):
            for t in range(LB):
                give[g][j, t] = terms_of(j * LB + t).astype(jnp.bfloat16)
            give_copy(g, j).start()
            return carry

        lax.fori_loop(0, inner, owner, 0)
        for t in range(LB):
            vacc[g, t] = terms_of(inner * LB + t)

    def value_copy(g, dz, dc):
        pz, pc = mate(dz, dc)
        return remote(
            value[g].at[member],
            value[g].at[member],
            val_s.at[g, dz * 2 + dc],
            val_r.at[g, dz * 2 + dc],
            device(zh * 2 + pz, xlo, pc, y, xhi),
        )

    def value_arrival(g, dz, dc):
        sz, sc = mate(dz, dc)
        return remote(
            value[g].at[sz * 2 + sc],
            value[g].at[sz * 2 + sc],
            val_s.at[g, dz * 2 + dc],
            val_r.at[g, dz * 2 + dc],
            device(zh * 2 + sz, xlo, sc, y, xhi),
        )

    def own(g):
        for d in range(1, 8):

            @pl.when(inner + d < 8)
            def _():
                give_arrival(g, d).wait_recv()
                vacc[g] += came[g][d - 1].astype(jnp.float32)

        value[g][member] = vacc[g].reshape(LB * BLK, HD).astype(jnp.bfloat16)
        for dz, dc in mates:
            value_copy(g, dz, dc).start()

    place_of = (y, x)

    def along(u, at_):
        return (outer, at_ * 2 + xhi) if u == 0 else across(at_)

    def part_copy(g, u, to):
        return remote(
            part[g].at[u, to],
            part_in[g].at[u, place_of[u]],
            p1_s.at[g, u * 4 + to],
            p1_r.at[g, u * 4 + place_of[u]],
            along(u, to),
        )

    def part_arrival(g, u, src):
        return remote(
            part[g].at[u, src],
            part_in[g].at[u, src],
            p1_s.at[g, u * 4 + src],
            p1_r.at[g, u * 4 + src],
            along(u, src),
        )

    def inputs_here():
        for load in x_loads:
            load.wait()
        for blk in range(8):
            xb_arrival(blk).wait_recv()
            for dz, dc in mates:
                xa_arrival(blk, dz, dc).wait_recv()

    def term_of(low_, wide):
        term = lax.dot_general(
            low_, wide, (((0,), (0,)), ((), ())), preferred_element_type=jnp.float32
        )
        return term.T.astype(jnp.bfloat16)

    def multiply(g):
        for dz, dc in mates:
            value_arrival(g, dz, dc).wait_recv()
        four = value[g][...].reshape(4 * LB * BLK, HD)
        two = value[g][pl.ds(2 * zl, 2)].reshape(2 * LB * BLK, HD)
        for to in range(4):
            wide = jnp.concatenate([xa_ref[2 * to], xa_ref[2 * to + 1]], axis=-1)
            rows = term_of(four, wide.reshape(4 * LB * BLK, 256)).reshape(4, 2, 32, HD)
            part[g][0, to, :, 2] = rows[:, 0]
            for at_ in range(4):
                part[g][1, at_, to, 2] = rows[at_, 1]
            for hi in range(2):
                rows = term_of(two, xb_ref[2 * to + hi].reshape(2 * LB * BLK, 256))
                rows = rows.reshape(2, 2, 2, 32, HD)
                for lo in range(2):
                    part[g][0, to, 2 * hi + lo, pl.ds(0, 2)] = rows[0, lo]
                    part[g][1, 2 * hi + lo, to, pl.ds(0, 2)] = rows[1, lo]
            send_part(g, 0, to)
        for to in range(4):
            send_part(g, 1, to)

    def send_part(g, u, to):
        @pl.when(place_of[u] != to)
        def _():
            part_copy(g, u, to).start()

        @pl.when(place_of[u] == to)
        def _():
            part_in[g][u, to] = part[g][u, to]

    def mid_copy(g, u, d):
        to = lax.rem(place_of[1 - u] + d, 4)
        return remote(
            mid[g].at[u, to],
            mid_in[g].at[u, d],
            p2_s.at[g, u * 4 + d],
            p2_r.at[g, u * 4 + d],
            along(1 - u, to),
        )

    def mid_arrival(g, u, d):
        src = lax.rem(place_of[1 - u] + 4 - d, 4)
        return remote(
            mid[g].at[u, src],
            mid_in[g].at[u, d],
            p2_s.at[g, u * 4 + d],
            p2_r.at[g, u * 4 + d],
            along(1 - u, src),
        )

    def sum_first(g):
        for u in range(2):
            for src in range(4):

                @pl.when(place_of[u] != src)
                def _():
                    part_arrival(g, u, src).wait_recv()

            terms = [part_in[g][u, k].astype(jnp.float32) for k in range(4)]
            total = (terms[0] + terms[1]) + (terms[2] + terms[3])
            mid[g][u] = total.astype(MID)
            for d in range(1, 4):
                mid_copy(g, u, d).start()

    def low_target(u, k):
        return (4 * zl + core, u) if k == 2 else (4 * core + 2 + u, k)

    def low_copy(g, u, k):
        to_z, to_core = low_target(u, k)
        return remote(
            low[g].at[u, k],
            low_in[g].at[z],
            p3_s.at[g, u * 3 + k],
            p3_r.at[g, z],
            device(to_z, xlo, to_core, y, xhi),
        )

    def low_stays(u, k):
        to_z, to_core = low_target(u, k)
        return (to_z == z) & (to_core == core)

    wide_z = lax.rem(z, 4) >= 2
    from_core = jnp.where(wide_z, z // 4, lax.rem(z, 2))

    def low_comes(src):
        return wide_z | (src % 2 == z // 4)

    def low_is_own(src):
        return (src == z) & (from_core == core)

    def low_arrival(g, src):
        return remote(
            low[g].at[0, 0],
            low_in[g].at[src],
            p3_s.at[g, 0],
            p3_r.at[g, src],
            device(src, xlo, from_core, y, xhi),
        )

    def sum_second(g):
        for u in range(2):
            total = mid[g][u, place_of[1 - u]].astype(jnp.float32)
            for d in range(1, 4):
                mid_arrival(g, u, d).wait_recv()
                total = total + mid_in[g][u, d].astype(jnp.float32)
            low[g][u] = total
            for k in range(3):

                @pl.when(jnp.logical_not(low_stays(u, k)))
                def _():
                    low_copy(g, u, k).start()

                @pl.when(low_stays(u, k))
                def _():
                    low_in[g][z] = low[g][u, k]

    def sum_z(g):
        column = pl.ds(g * HD, HD)
        out_ref[:, column] = jnp.zeros((32, HD), jnp.float32)
        for src in range(8):

            @pl.when(low_comes(src) & jnp.logical_not(low_is_own(src)))
            def _():
                low_arrival(g, src).wait_recv()

            @pl.when(low_comes(src))
            def _():
                out_ref[:, column] += low_in[g][src]

    def start_of(g):
        for d in range(1, 8):

            @pl.when(key_comes(d))
            def _():
                key_arrival(g, d).wait_recv()

        k_loads[g].wait()
        q_loads[g].wait()
        g_loads[g].wait()

    def next_keys(g):
        for d in range(1, 8):

            @pl.when(key_goes(d))
            def _():
                key_copy(g - 1, d).wait_send()
                key_copy(g, d).start()

    def step(g):
        start_of(g)
        attend(g)
        hand_out(g)
        if g + 2 < HK:
            next_keys(g + 2)

    next_keys(1)
    step(0)
    step(1)
    own(0)
    step(2)
    own(1)
    inputs_here()
    multiply(0)
    step(3)
    own(2)
    multiply(1)
    sum_first(0)
    own(3)
    multiply(2)
    sum_first(1)
    multiply(3)
    sum_second(0)
    sum_first(2)
    sum_second(1)
    sum_first(3)
    sum_second(2)
    sum_second(3)
    for g in range(HK):
        sum_z(g)

    for g in range(HK):
        for d in range(1, 8):

            if g + 1 == HK:

                @pl.when(key_goes(d))
                def _():
                    key_copy(g, d).wait_send()

            @pl.when(inner - d >= 0)
            def _():
                give_copy(g, inner - d).wait_send()

        for dz, dc in mates:
            value_copy(g, dz, dc).wait_send()
        for u in range(2):
            for to in range(4):

                @pl.when(place_of[u] != to)
                def _():
                    part_copy(g, u, to).wait_send()

            for d in range(1, 4):
                mid_copy(g, u, d).wait_send()
            for k in range(3):

                @pl.when(jnp.logical_not(low_stays(u, k)))
                def _():
                    low_copy(g, u, k).wait_send()

    for blk in range(8):
        xb_copy(blk).wait_send()
        for dz, dc in mates:
            xa_copy(blk, dz, dc).wait_send()


def body(inputs, queries, key_rows, out_grad, sel_blocks, block_mask):
    any_ref = pl.BlockSpec(memory_space=pl.ANY)
    smem = pl.BlockSpec(memory_space=pltpu.SMEM)
    bf16, f32 = jnp.bfloat16, jnp.float32
    dma = pltpu.SemaphoreType.DMA
    scratch = (
        [pltpu.VMEM((NB, BLK, HD), bf16)] * HK
        + [pltpu.VMEM((8, LB, BLK, HD), bf16)] * HK
        + [pltpu.VMEM((7, LB, BLK, HD), bf16)] * HK
        + [pltpu.VMEM((4, LB * BLK, HD), bf16)] * HK
        + [pltpu.VMEM((2, 4, 4, 3, 32, HD), bf16)] * HK
        + [pltpu.VMEM((2, 4, 4, 3, 32, HD), bf16)] * HK
        + [pltpu.VMEM((2, 4, 3, 32, HD), MID)] * HK
        + [pltpu.VMEM((2, 4, 3, 32, HD), MID)] * HK
        + [pltpu.VMEM((2, 3, 32, HD), f32)] * HK
        + [pltpu.VMEM((8, 32, HD), f32)] * HK
        + [
            pltpu.VMEM((HK, LB, BLK, 1024), bf16),
            pltpu.VMEM((HK, LB, BLK, 1024), bf16),
            pltpu.VMEM((8, 4, LB * BLK, 128), bf16),
            pltpu.VMEM((8, 2, LB * BLK, 256), bf16),
            pltpu.VMEM((4, 256, GROUP * BLK), f32),
            pltpu.VMEM((LB, SEL + 1, BLK, HD), f32),
            pltpu.VMEM((3, BLK, HD), f32),
            pltpu.VMEM((HK, LB, BLK, HD), f32),
            pltpu.SMEM((LB, NB), jnp.int32),
        ]
        + [
            dma((5, 8)),
            dma((HK, 8)),
            dma((HK, 8)),
            dma((4, 8)),
            dma((4, 8)),
            dma((8,)),
            dma((8,)),
            dma((HK, 8)),
            dma((HK, 8)),
            dma((HK, 4)),
            dma((HK, 4)),
        ]
        + [dma((HK, 8))] * 6
    )
    return pl.pallas_call(
        kernel,
        out_shape=jax.ShapeDtypeStruct((32, HK * HD), f32),
        in_specs=[any_ref, any_ref, any_ref, any_ref, smem, smem],
        out_specs=pl.BlockSpec(memory_space=pltpu.VMEM),
        scratch_shapes=scratch,
        compiler_params=pltpu.CompilerParams(
            collective_id=0, has_side_effects=True, vmem_limit_bytes=56 * 1024 * 1024
        ),
        cost_estimate=pl.CostEstimate(
            flops=6_500_000_000, bytes_accessed=9_000_000, transcendentals=8_400_000
        ),
    )(
        inputs,
        queries.reshape(LB, BLK, 4096),
        key_rows.reshape(LB, BLK, 512),
        out_grad.reshape(LB, BLK, 4096),
        sel_blocks,
        block_mask,
    )


def solution(mesh):
    placed = P(("outer", "inner"), None)
    return jax.shard_map(
        body, mesh=mesh, in_specs=(placed,) * 6, out_specs=P(("inner", "outer"), None), check_vma=False
    )
```

time: 147 us -> 90.9 us (0.62)
  Pallas kernels: 146 us -> 89.2 us
    pallas_call x1, Pallas kernels: 146 us -> 89.2 us  [body(): pl.pallas_call(kernel, out_shape=jax.ShapeDtypeStruct((32, HK * HD), f32)...]
where the time goes in v2:
time: 90.9 us; the launch traced here: 90.7 us
  Pallas kernels  89.2 us (98%)
  local copies, waits for them, and re-layouts  1.47 us (2%)
    pallas_call x1, Pallas kernels, body(): pl.pallas_call(kernel, out_shape=jax.ShapeDtypeStruct((32, HK * HD), f32)...  89.2 us

profile of v2, /device:TPU:1, one launch (start us, length us, event | category | flops | bytes accessed | tf_op | source)
XLA Modules:
  0.0 90.7 jit_solution(3339483483768772758)
XLA Ops:
  0.0 89.2 %shard_map.64 = f32[32,512]{1,0:T(8,128)} custom-call(bf16[256,8192]{1,0:T(8,128)(2,1)} %inputs.1, bf16[4,64,4096]{2,1,0:T(8,128)(2,1)} %bitcast.3, bf16[4,64,512]{2,1,0:T(8,128)(2,1)} %bitcast.5, bf16[4,64,4096]{2,1,0:T(8,128)(2,1)} %bitcast.4, s32[4,16]{1,0:T(4,128)} %sel.1, s32[4,16]{1,0:T(4,128)} %mask.1), custom_call_target="tpu_custom_call" | custom-call | flops 6499999744 | bytes 9000000 | tf_op jit(solution)/shard_map/pallas_call | solution.py:613
  89.3 1.5 %copy.8 = f32[32,512]{1,0:T(8,128)} copy(f32[32,512]{1,0:T(8,128)} %shard_map.64) | data formatting | bytes 131072

commit v3 on v2

--- a/solution.py
+++ b/solution.py
@@ -19,7 +19,7 @@
 MID = jnp.bfloat16
 
 
-def kernel(inputs, queries, key_rows, out_grad, sel, mask, out_ref, *scratch):
+def kernel(inputs, queries, key_rows, out_grad, sel_in, mask_in, out_ref, *scratch):
     scratch = list(scratch)
 
     def take(count):
@@ -37,7 +37,7 @@
     mid_in = take(HK)
     low = take(HK)
     low_in = take(HK)
-    (q_ref, g_ref, xa_ref, xb_ref, st_ref, contrib, bias, vacc, inverse) = take(9)
+    (q_ref, g_ref, xa_ref, xb_ref, st_ref, contrib, bias, vacc, inverse, sel, mask) = take(11)
     (loc, key_s, key_r, xa_s, xa_r, xb_s, xb_r, give_s, give_r, val_s, val_r) = take(11)
     (p1_s, p1_r, p2_s, p2_r, p3_s, p3_r) = take(6)
 
@@ -106,6 +106,12 @@
             pltpu.make_async_copy(columns_a(blk, member), xa_ref.at[blk, member], loc.at[3, blk]),
             pltpu.make_async_copy(columns_b(blk, core), xb_ref.at[blk, core], loc.at[4, blk]),
         ]
+    choices = [
+        pltpu.make_async_copy(sel_in, sel, loc.at[0, 4]),
+        pltpu.make_async_copy(mask_in, mask, loc.at[0, 5]),
+    ]
+    for choice in choices:
+        choice.start()
     for g in range(HK):
         k_loads[g].start()
         q_loads[g].start()
@@ -194,6 +200,9 @@
         xb_copy(blk).start()
     for load in x_loads:
         load.start()
+
+    for choice in choices:
+        choice.wait()
 
     for qb in range(LB):
         named = [jnp.where(mask[qb, s] == 1, sel[qb, s], -1) for s in range(SEL)]
@@ -457,7 +466,7 @@
             for d in range(1, 4):
                 mid_arrival(g, u, d).wait_recv()
                 total = total + mid_in[g][u, d].astype(jnp.float32)
-            low[g][u] = total
+            low[g][u] = total.astype(MID)
             for k in range(3):
 
                 @pl.when(jnp.logical_not(low_stays(u, k)))
@@ -479,7 +488,7 @@
 
             @pl.when(low_comes(src))
             def _():
-                out_ref[:, column] += low_in[g][src]
+                out_ref[:, column] += low_in[g][src].astype(jnp.float32)
 
     def start_of(g):
         for d in range(1, 8):
@@ -508,69 +517,84 @@
             next_keys(g + 2)
 
     next_keys(1)
+    def early_left(g):
+        for d in range(1, 8):
+            if g + 1 == HK:
+
+                @pl.when(key_goes(d))
+                def _():
+                    key_copy(g, d).wait_send()
+
+            @pl.when(inner - d >= 0)
+            def _():
+                give_copy(g, inner - d).wait_send()
+
+        for dz, dc in mates:
+            value_copy(g, dz, dc).wait_send()
+
+    def inputs_left():
+        for blk in range(8):
+            xb_copy(blk).wait_send()
+            for dz, dc in mates:
+                xa_copy(blk, dz, dc).wait_send()
+
+    def sums_left(g):
+        for u in range(2):
+            for to in range(4):
+
+                @pl.when(place_of[u] != to)
+                def _():
+                    part_copy(g, u, to).wait_send()
+
+            for d in range(1, 4):
+                mid_copy(g, u, d).wait_send()
+
+    def low_left(g):
+        for u in range(2):
+            for k in range(3):
+
+                @pl.when(jnp.logical_not(low_stays(u, k)))
+                def _():
+                    low_copy(g, u, k).wait_send()
+
     step(0)
     step(1)
     own(0)
     step(2)
     own(1)
+    step(3)
     inputs_here()
     multiply(0)
-    step(3)
+    multiply(1)
     own(2)
-    multiply(1)
     sum_first(0)
     own(3)
+    inputs_left()
     multiply(2)
     sum_first(1)
+    sum_second(0)
     multiply(3)
-    sum_second(0)
     sum_first(2)
     sum_second(1)
+    for g in range(HK):
+        early_left(g)
     sum_first(3)
     sum_second(2)
+    for g in range(3):
+        sums_left(g)
+    sum_z(0)
+    sum_z(1)
     sum_second(3)
-    for g in range(HK):
-        sum_z(g)
-
-    for g in range(HK):
-        for d in range(1, 8):
-
-            if g + 1 == HK:
-
-                @pl.when(key_goes(d))
-                def _():
-                    key_copy(g, d).wait_send()
-
-            @pl.when(inner - d >= 0)
-            def _():
-                give_copy(g, inner - d).wait_send()
-
-        for dz, dc in mates:
-            value_copy(g, dz, dc).wait_send()
-        for u in range(2):
-            for to in range(4):
-
-                @pl.when(place_of[u] != to)
-                def _():
-                    part_copy(g, u, to).wait_send()
-
-            for d in range(1, 4):
-                mid_copy(g, u, d).wait_send()
-            for k in range(3):
-
-                @pl.when(jnp.logical_not(low_stays(u, k)))
-                def _():
-                    low_copy(g, u, k).wait_send()
-
-    for blk in range(8):
-        xb_copy(blk).wait_send()
-        for dz, dc in mates:
-            xa_copy(blk, dz, dc).wait_send()
+    sums_left(3)
+    sum_z(2)
+    for g in range(3):
+        low_left(g)
+    sum_z(3)
+    low_left(3)
 
 
 def body(inputs, queries, key_rows, out_grad, sel_blocks, block_mask):
     any_ref = pl.BlockSpec(memory_space=pl.ANY)
-    smem = pl.BlockSpec(memory_space=pltpu.SMEM)
     bf16, f32 = jnp.bfloat16, jnp.float32
     dma = pltpu.SemaphoreType.DMA
     scratch = (
@@ -582,8 +606,8 @@
         + [pltpu.VMEM((2, 4, 4, 3, 32, HD), bf16)] * HK
         + [pltpu.VMEM((2, 4, 3, 32, HD), MID)] * HK
         + [pltpu.VMEM((2, 4, 3, 32, HD), MID)] * HK
-        + [pltpu.VMEM((2, 3, 32, HD), f32)] * HK
-        + [pltpu.VMEM((8, 32, HD), f32)] * HK
+        + [pltpu.VMEM((2, 3, 32, HD), MID)] * HK
+        + [pltpu.VMEM((8, 32, HD), MID)] * HK
         + [
             pltpu.VMEM((HK, LB, BLK, 1024), bf16),
             pltpu.VMEM((HK, LB, BLK, 1024), bf16),
@@ -594,6 +618,8 @@
             pltpu.VMEM((3, BLK, HD), f32),
             pltpu.VMEM((HK, LB, BLK, HD), f32),
             pltpu.SMEM((LB, NB), jnp.int32),
+            pltpu.SMEM((LB, SEL), jnp.int32),
+            pltpu.SMEM((LB, SEL), jnp.int32),
         ]
         + [
             dma((5, 8)),
@@ -613,7 +639,7 @@
     return pl.pallas_call(
         kernel,
         out_shape=jax.ShapeDtypeStruct((32, HK * HD), f32),
-        in_specs=[any_ref, any_ref, any_ref, any_ref, smem, smem],
+        in_specs=[any_ref] * 6,
         out_specs=pl.BlockSpec(memory_space=pltpu.VMEM),
         scratch_shapes=scratch,
         compiler_params=pltpu.CompilerParams(

time: 90.9 us -> 88.3 us (0.971)
  Pallas kernels: 89.2 us -> 86.7 us
    pallas_call x1, Pallas kernels: 89.2 us -> 86.7 us  [body(): pl.pallas_call(kernel, out_shape=jax.ShapeDtypeStruct((32, HK * HD), f32)...]
where the time goes in v3:
time: 88.3 us; the launch traced here: 88.1 us
  Pallas kernels  86.7 us (98%)
  local copies, waits for them, and re-layouts  1.47 us (2%)
    pallas_call x1, Pallas kernels, body(): pl.pallas_call(kernel, out_shape=jax.ShapeDtypeStruct((32, HK * HD), f32)...  86.7 us

profile of v3, /device:TPU:1, one launch (start us, length us, event | category | flops | bytes accessed | tf_op | source)
XLA Modules:
  0.0 88.1 jit_solution(8250254264532111146)
XLA Ops:
  0.0 86.7 %shard_map.64 = f32[32,512]{1,0:T(8,128)} custom-call(bf16[256,8192]{1,0:T(8,128)(2,1)} %inputs.1, bf16[4,64,4096]{2,1,0:T(8,128)(2,1)} %bitcast.3, bf16[4,64,512]{2,1,0:T(8,128)(2,1)} %bitcast.5, bf16[4,64,4096]{2,1,0:T(8,128)(2,1)} %bitcast.4, s32[4,16]{1,0:T(4,128)} %sel_in.1, s32[4,16]{1,0:T(4,128)} %mask_in.1), custom_call_target="tpu_custom_call" | custom-call | flops 6499999744 | bytes 9000000 | tf_op jit(solution)/shard_map/pallas_call | solution.py:639
  86.7 1.5 %copy.8 = f32[32,512]{1,0:T(8,128)} copy(f32[32,512]{1,0:T(8,128)} %shard_map.64) | data formatting | bytes 131072

commit v4 on v3

--- a/solution.py
+++ b/solution.py
@@ -321,7 +321,7 @@
                 vacc[g] += came[g][d - 1].astype(jnp.float32)
 
         value[g][member] = vacc[g].reshape(LB * BLK, HD).astype(jnp.bfloat16)
-        for dz, dc in mates:
+        for dz, dc in mates[::-1]:
             value_copy(g, dz, dc).start()
 
     place_of = (y, x)
@@ -362,22 +362,24 @@
         return term.T.astype(jnp.bfloat16)
 
     def multiply(g):
-        for dz, dc in mates:
-            value_arrival(g, dz, dc).wait_recv()
+        value_arrival(g, 0, 1).wait_recv()
+        two = value[g][pl.ds(2 * zl, 2)].reshape(2 * LB * BLK, HD)
+        for blk in range(8):
+            to, hi = blk // 2, blk % 2
+            rows = term_of(two, xb_ref[blk].reshape(2 * LB * BLK, 256))
+            rows = rows.reshape(2, 2, 2, 32, HD)
+            for lo in range(2):
+                part[g][0, to, 2 * hi + lo, pl.ds(0, 2)] = rows[0, lo]
+                part[g][1, 2 * hi + lo, to, pl.ds(0, 2)] = rows[1, lo]
+        for dc in range(2):
+            value_arrival(g, 1, dc).wait_recv()
         four = value[g][...].reshape(4 * LB * BLK, HD)
-        two = value[g][pl.ds(2 * zl, 2)].reshape(2 * LB * BLK, HD)
         for to in range(4):
             wide = jnp.concatenate([xa_ref[2 * to], xa_ref[2 * to + 1]], axis=-1)
             rows = term_of(four, wide.reshape(4 * LB * BLK, 256)).reshape(4, 2, 32, HD)
             part[g][0, to, :, 2] = rows[:, 0]
             for at_ in range(4):
                 part[g][1, at_, to, 2] = rows[at_, 1]
-            for hi in range(2):
-                rows = term_of(two, xb_ref[2 * to + hi].reshape(2 * LB * BLK, 256))
-                rows = rows.reshape(2, 2, 2, 32, HD)
-                for lo in range(2):
-                    part[g][0, to, 2 * hi + lo, pl.ds(0, 2)] = rows[0, lo]
-                    part[g][1, 2 * hi + lo, to, pl.ds(0, 2)] = rows[1, lo]
             send_part(g, 0, to)
         for to in range(4):
             send_part(g, 1, to)

time: 88.3 us -> 88.5 us (level)
  no operation moved by 1% of the time
where the time goes in v4:
time: 88.5 us; the launch traced here: 88.3 us
  Pallas kernels  86.9 us (98%)
  local copies, waits for them, and re-layouts  1.47 us (2%)
    pallas_call x1, Pallas kernels, body(): pl.pallas_call(kernel, out_shape=jax.ShapeDtypeStruct((32, HK * HD), f32)...  86.9 us

profile of v4, /device:TPU:1, one launch (start us, length us, event | category | flops | bytes accessed | tf_op | source)
XLA Modules:
  0.0 88.3 jit_solution(16037023835686971419)
XLA Ops:
  0.0 86.9 %shard_map.64 = f32[32,512]{1,0:T(8,128)} custom-call(bf16[256,8192]{1,0:T(8,128)(2,1)} %inputs.1, bf16[4,64,4096]{2,1,0:T(8,128)(2,1)} %bitcast.3, bf16[4,64,512]{2,1,0:T(8,128)(2,1)} %bitcast.5, bf16[4,64,4096]{2,1,0:T(8,128)(2,1)} %bitcast.4, s32[4,16]{1,0:T(4,128)} %sel_in.1, s32[4,16]{1,0:T(4,128)} %mask_in.1), custom_call_target="tpu_custom_call" | custom-call | flops 6499999744 | bytes 9000000 | tf_op jit(solution)/shard_map/pallas_call | solution.py:641
  86.9 1.5 %copy.8 = f32[32,512]{1,0:T(8,128)} copy(f32[32,512]{1,0:T(8,128)} %shard_map.64) | data formatting | bytes 131072
